TPU v7x, 512 devices: a whole 4x4x16 slice. The times are simulated.
512 devices in a mesh: row: 16 (over z), col: 32 (over x, y, core).
Axes of the slice: x: 4, y: 4, z: 16, core: 2. Of those that a mesh axis runs over, the one named last changes fastest.
Arguments:
- tensor: float32 [8, 2048, 8192], P(None, 'row', 'col'), may hold values from -12288 to 12288
- factor_b: float32 [256, 8192], P('row', 'col'), may hold values from -6 to 6
- factor_c: float32 [8, 256], replicated, may hold values from -6 to 6
Outputs:
- new_a: float32 [2048, 256], P(('row', 'col'))
- new_b: float32 [256, 8192], P('row', 'col')
- new_c: float32 [8, 256], replicated
All inputs are finite; a program needn't handle non-finite values.
Results may differ from a plain program's by a relative error of at most 0.0001.
Values sent between devices are 32-bit elements; how exact they have to be, the bound alone decides.
A program may use at most 64 MiB of HBM per device.

v0:
```python
import jax
import jax.numpy as jnp
from jax import lax
from jax.sharding import PartitionSpec as P

highest = lax.Precision.HIGHEST
epsilon = 1e-06


def product(left, right):
    return jnp.dot(left, right, precision=highest, preferred_element_type=jnp.float32)


def product_first(left, right):
    return lax.dot_general(
        left, right, (((0,), (0,)), ((), ())), precision=highest, preferred_element_type=jnp.float32
    )


def solve_rows(right_side, system):
    lower_factor = jnp.linalg.cholesky(system)
    halfway = lax.linalg.triangular_solve(
        lower_factor, right_side, left_side=False, lower=True, transpose_a=True
    )
    return lax.linalg.triangular_solve(
        lower_factor, halfway, left_side=False, lower=True, transpose_a=False
    )


def column_scale(gram_raw, count):
    return jnp.sqrt(jnp.diagonal(gram_raw) / count + epsilon)


def scaled_gram(gram_raw, scale):
    return gram_raw / (scale[:, None] * scale[None, :])


def mode_one(slab_block, block_b, factor_c):
    summed = jnp.zeros((slab_block.shape[1], block_b.shape[1]), jnp.float32)
    for member in range(slab_block.shape[0]):
        summed = summed + product(slab_block[member], block_b) * factor_c[member]
    return summed


def on_device(tensor, factor_b, factor_c):
    rows_a = tensor.shape[1]
    rows_b = tensor.shape[2]
    total_a = rows_a * lax.axis_size("row")
    total_b = rows_b * lax.axis_size("col")
    gram_c = product(factor_c.T, factor_c)
    block_b = lax.all_gather(factor_b, "row", axis=0, tiled=True)
    gram_b = lax.psum(product(factor_b.T, factor_b), ("row", "col"))
    system_a = gram_b * gram_c
    mttkrp_a = lax.psum_scatter(
        mode_one(tensor, block_b, factor_c), "col", scatter_dimension=0, tiled=True
    )
    raw_a = solve_rows(mttkrp_a, system_a)
    gram_raw_a = lax.psum(product(raw_a.T, raw_a), ("row", "col"))
    scale_a = column_scale(gram_raw_a, total_a)
    new_a = raw_a / scale_a
    block_a = lax.all_gather(new_a, "col", axis=0, tiled=True)
    gram_a = scaled_gram(gram_raw_a, scale_a)
    system_b = gram_a * gram_c
    partial_b = jnp.zeros((rows_b, block_a.shape[1]), jnp.float32)
    for member in range(tensor.shape[0]):
        partial_b = partial_b + product_first(tensor[member], block_a) * factor_c[member]
    mttkrp_b = lax.psum_scatter(partial_b, "row", scatter_dimension=0, tiled=True)
    raw_b = solve_rows(mttkrp_b, system_b)
    gram_raw_b = lax.psum(product(raw_b.T, raw_b), ("row", "col"))
    scale_b = column_scale(gram_raw_b, total_b)
    new_b = raw_b / scale_b
    block_next = lax.all_gather(new_b, "row", axis=0, tiled=True)
    gram_next_b = scaled_gram(gram_raw_b, scale_b)
    partial_c = jnp.stack(
        [
            jnp.sum(product(tensor[member], block_next) * block_a, axis=0)
            for member in range(tensor.shape[0])
        ]
    )
    mttkrp_c = lax.psum(partial_c, ("row", "col"))
    new_c = solve_rows(mttkrp_c, gram_a * gram_next_b)
    return (new_a, new_b, new_c)


def solution(mesh):
    placed = (P(None, "row", "col"), P("row", "col"), P())
    return jax.shard_map(
        on_device,
        mesh=mesh,
        in_specs=placed,
        out_specs=(P(("row", "col"), None), P("row", "col"), P()),
        check_vma=False,
    )
```

profile of v0, /device:TPU:1, one launch (start us, length us, event | category | flops | bytes accessed | tf_op | source)
XLA Modules:
  0.0 1860.7 jit_solution(112213277089431246)
XLA Ops:
  7.2 1.9 fusion.125
  9.2 30.7 %all_gather.9 = f32[256,256]{1,0:T(8,128)S(1)} all-gather(f32[16,256]{1,0:T(8,128)} %param.5), channel_id=1, replica_groups=mesh['row'=16,'col'=32] {'row'}, dimensions={0}, use_global_device_ids=true | all-gather | bytes 278528 | tf_op jit(solution)/shard_map/all_gather | solution.py:51
  39.9 1.0 fusion.123
  40.9 1.2 convolution_multiply_fusion.15
  43.9 0.9 fusion.16
  45.2 1.3 dynamic-slice.9
  47.1 426.9 %all-reduce.7.cloned.1.call-done = f32[256,256]{0,1:T(8,128)} async-done(((f32[256,256]{0,1:T(8,128)}), f32[256,256]{0,1:T(8,128)}) %all-reduce.7.cloned.1.call-update) | async-done | bytes 262160 | tf_op jit(solution)/shard_map/psum | solution.py:52
  474.1 1.4 fusion.124
  475.6 11.7 cholesky.172
  487.4 9.8 custom-call.32
  497.7 11.7 cholesky.189
  509.5 0.7 compare_reduce_fusion.4
  511.7 4.6 while.3
  512.8 1.4 bitcast_dynamic-update-slice_fusion.6
  514.9 1.4 bitcast_dynamic-update-slice_fusion.6
  516.3 19.7 %custom-call.23 = f32[2,128,128]{1,2,0:T(8,128)S(1)} custom-call(f32[2,128,128]{2,1,0:T(8,128)S(1)} %get-tuple-element.11), custom_call_target="InvertDiagBlocksLowerTriangular" | custom-call | tf_op jit(solution)/shard_map/triangular_solve | solution.py:22
  536.0 69.4 %all-reduce.13.cloned.1.call-done = f32[128,256]{1,0:T(8,128)} async-done(((f32[128,256]{1,0:T(8,128)}), f32[128,256]{1,0:T(8,128)}) %all-reduce.13.cloned.1.call-update) | async-done | bytes 131088
  605.4 0.8 fusion.92
  606.2 0.9 convolution_subtract_fusion.8
  607.9 1.2 fusion.115
  609.1 457.1 %all-reduce.9.cloned.1.call-done = f32[256,256]{0,1:T(8,128)} async-done(((f32[256,256]{0,1:T(8,128)}), f32[256,256]{0,1:T(8,128)}) %all-reduce.9.cloned.1.call-update) | async-done | bytes 262160 | tf_op jit(solution)/shard_map/psum | solution.py:58
  1066.3 2.7 gather_fusion
  1069.3 11.7 cholesky.206
  1081.1 9.8 custom-call.33
  1091.4 11.7 cholesky.223
  1104.4 26.3 %all-gather = f32[32,4,256]{2,1,0:T(4,128)S(1)} all-gather(f32[1,4,256]{2,1,0:T(4,128)S(1)} %bitcast.264), channel_id=1, replica_groups=mesh['row'=16,'col'=32] {'col'}, dimensions={0}, use_global_device_ids=true | all-gather | bytes 135168 | tf_op jit(solution)/shard_map/all_gather | solution.py:61
  1134.2 0.8 copy.35
  1136.3 3.8 while.4
  1137.0 1.3 bitcast_dynamic-update-slice_fusion.7
  1138.9 1.3 bitcast_dynamic-update-slice_fusion.7
  1140.2 19.7 %custom-call.24 = f32[2,128,128]{1,2,0:T(8,128)S(1)} custom-call(f32[2,128,128]{2,1,0:T(8,128)S(1)} %get-tuple-element.19), custom_call_target="InvertDiagBlocksLowerTriangular" | custom-call | tf_op jit(solution)/shard_map/triangular_solve | solution.py:22
  1159.9 25.8 %reduce-scatter.4.cloned.1.call-done = f32[16,256]{1,0:T(8,128)} async-done(((f32[256,256]{1,0:T(8,128)}), f32[16,256]{1,0:T(8,128)}) %reduce-scatter.4.cloned.1.call-update) | async-done | bytes 16400 | tf_op jit(solution)/shard_map/reduce_scatter | solution.py:67
  1185.7 0.9 fusion.96
  1187.6 1.2 fusion.111
  1188.8 466.6 %all-reduce.11.cloned.1.call-done = f32[256,256]{0,1:T(8,128)} async-done(((f32[256,256]{0,1:T(8,128)}), f32[256,256]{0,1:T(8,128)}) %all-reduce.11.cloned.1.call-update) | async-done | bytes 262160 | tf_op jit(solution)/shard_map/psum | solution.py:69
  1655.4 2.6 gather_fusion.1
  1658.1 23.9 %all_gather.11 = f32[256,256]{1,0:T(8,128)S(1)} all-gather(f32[16,256]{1,0:T(8,128)S(1)} %fusion.110), channel_id=1, replica_groups=mesh['row'=16,'col'=32] {'row'}, dimensions={0}, use_global_device_ids=true | all-gather | bytes 278528 | tf_op jit(solution)/shard_map/all_gather | solution.py:72
  1685.5 11.7 cholesky.240
  1697.3 9.8 custom-call.34
  1707.6 11.9 cholesky.257
  1719.5 0.7 compare_reduce_fusion.1
  1722.2 4.1 while.5
  1722.2 0.7 fusion.180
  1722.9 1.3 bitcast_dynamic-update-slice_fusion.8
  1724.3 0.7 fusion.180
  1724.9 1.3 bitcast_dynamic-update-slice_fusion.8
  1726.3 19.7 %custom-call.25 = f32[2,128,128]{1,2,0:T(8,128)S(1)} custom-call(f32[2,128,128]{2,1,0:T(8,128)S(1)} %get-tuple-element.27), custom_call_target="InvertDiagBlocksLowerTriangular" | custom-call | tf_op jit(solution)/shard_map/triangular_solve | solution.py:22
  1746.0 106.1 %psum.31 = f32[8,256]{1,0:T(8,128)S(1)} all-reduce(f32[8,256]{1,0:T(8,128)S(1)} %stack.35), channel_id=1, replica_groups=mesh['row'=16,'col'=32] {'row','col'}, use_global_device_ids=true, to_apply=%region_17.19 | all-reduce | flops 2048 | bytes 16384 | tf_op jit(solution)/shard_map/psum | solution.py:80
  (116 shorter events, 19.5 us)
Async XLA Ops:
  7.2 34.9 %copy-start = (f32[8,128,256]{2,1,0:T(8,128)S(1)}, f32[8,128,256]{2,1,0:T(8,128)}, u32[]{:S(2)}) copy-start(f32[8,128,256]{2,1,0:T(8,128)} %param.4) | copy-start | bytes 3145732
  7.2 466.9 %all-reduce.7.cloned.1.call-start = ((), (), s32[]{:S(2)}) async-start(), calls=%async_computation.1 | async-start | bytes 524288 | tf_op jit(solution)/shard_map/psum | solution.py:52
  9.2 596.2 %all-reduce.13.cloned.1.call-start = ((), (), s32[]{:S(2)}) async-start(), calls=%async_computation.5 | async-start | bytes 262144
  44.8 1021.4 %all-reduce.9.cloned.1.call-start = ((), (), s32[]{:S(2)}) async-start(), calls=%async_computation.2 | async-start | bytes 524288 | tf_op jit(solution)/shard_map/psum | solution.py:58
  45.2 428.9 %copy-start.3 = (f32[8,256]{1,0:T(8,128)S(1)}, f32[8,256]{1,0:T(8,128)}, u32[]{:S(2)}) copy-start(f32[8,256]{1,0:T(8,128)} %param.6) | copy-start | bytes 24580
  609.1 576.6 %reduce-scatter.4.cloned.1.call-start = ((), (), s32[]{:S(2)}) async-start(), calls=%async_computation.4 | async-start | bytes 278528 | tf_op jit(solution)/shard_map/reduce_scatter | solution.py:67
  1066.3 2.7 copy-start.1
  1069.0 35.4 %copy-start.5 = (f32[4,256]{1,0:T(4,128)}, f32[4,256]{1,0:T(4,128)S(1)}, u32[]{:S(2)}) copy-start(f32[4,256]{1,0:T(4,128)S(1)} %fusion.114) | copy-start | bytes 12292
  1135.1 520.4 %all-reduce.11.cloned.1.call-start = ((), (), s32[]{:S(2)}) async-start(), calls=%async_computation.3 | async-start | bytes 524288 | tf_op jit(solution)/shard_map/psum | solution.py:69
  1185.7 0.9 copy-start.6
  1658.0 23.9 %copy-start.4 = (f32[16,256]{1,0:T(8,128)}, f32[16,256]{1,0:T(8,128)S(1)}, u32[]{:S(2)}) copy-start(f32[16,256]{1,0:T(8,128)S(1)} %fusion.110) | copy-start | bytes 49156
  1684.2 1.0 copy-start.2
Sparse Core Ops, SparseCore 0:
  13.4 460.5 all-reduce.6
  477.6 127.7 all-reduce.12
  610.8 455.3 all-reduce.8
  1135.2 50.4 reduce-scatter.3
  1191.0 464.4 all-reduce.10
where the time goes:
time: 1860 us
  waiting for transfers between devices  1450 us (78%)
  blocking collectives  187 us (10%)
  other arithmetic  164 us (9%)
  matrix products  22.3 us (1%)
  local copies, waits for them, and re-layouts  21.5 us (1%)
  between operations  19 us (1%)
    psum x1, waiting for transfers between devices, on_device(): gram_raw_b = lax.psum(product(raw_b.T, raw_b), ('row', 'col'))  467 us
    psum x1, waiting for transfers between devices, on_device(): gram_raw_a = lax.psum(product(raw_a.T, raw_a), ('row', 'col'))  457 us
    psum x1, waiting for transfers between devices, on_device(): gram_b = lax.psum(product(factor_b.T, factor_b), ('row', 'col'))  427 us
    psum x1, blocking collectives, on_device(): mttkrp_c = lax.psum(partial_c, ('row', 'col'))  106 us
    another operation x20, other arithmetic, solve_rows(): lower_factor = jnp.linalg.cholesky(system)  103 us
    unnamed x6, waiting for transfers between devices  69.5 us
    another operation x7, other arithmetic, solve_rows(): lax.linalg.triangular_solve(lower_factor, right_side, left_side=False, lo...  59.1 us
  transfers between devices with their start and end apart: 5, of which 5 were waited for; matrix products, arithmetic and copies ran while one was open for 5% of the time, Pallas kernels for 0%

commit v1 on v0

v1 whole, which is shorter than its diff:
```python
import functools

import jax
import jax.numpy as jnp
from jax import lax
from jax.experimental import pallas as pl
from jax.experimental.pallas import tpu as pltpu
from jax.sharding import PartitionSpec as P

f32 = jnp.float32
bf16 = jnp.bfloat16
highest = lax.Precision.HIGHEST
epsilon = 1e-06
EXCHANGES = 19


def dot(left, right):
    return jnp.dot(left, right, precision=highest, preferred_element_type=f32)


def lane_of(tile, index):
    return jnp.take_along_axis(tile, jnp.full(tile.shape, index, jnp.int32), axis=1)


def row_of(tile, k):
    return jnp.broadcast_to(tile[k : k + 1], tile.shape)


def added(parts):
    while len(parts) > 1:
        parts = [a + b for a, b in zip(parts[::2], parts[1::2])] + parts[len(parts) & ~1 :]
    return parts[0]


def pivot_panel(tile, p):
    lane = lax.broadcasted_iota(jnp.int32, (8, 128), 1)
    sub = lax.broadcasted_iota(jnp.int32, (8, 128), 0)
    d = [lane_of(tile, p * 8 + k) for k in range(8)]
    for j in range(8):
        here = sub == j
        c = jnp.where(here, -1.0, d[j]) * (1.0 / row_of(d[j], j))
        d = [-c if k == j else jnp.where(here, 0.0, d[k]) - c * row_of(d[k], j) for k in range(8)]
    rows = jnp.where(lane // 8 == p, jnp.where(lane % 8 == sub, 1.0, 0.0), tile)
    return added([d[k] * row_of(rows, k) for k in range(8)])


def cleared(tile, p, pivot):
    lane = lax.broadcasted_iota(jnp.int32, (8, 128), 1)
    return jnp.where(lane // 8 == p, 0.0, tile) - added(
        [lane_of(tile, p * 8 + k) * row_of(pivot, k) for k in range(8)]
    )


def thirds(x):
    high = x.astype(bf16).astype(f32)
    rest = x - high
    middle = rest.astype(bf16).astype(f32)
    return high, middle, rest - middle


def outer(left, right):
    lh, lm, ll = thirds(left)
    rh, rm, rl = thirds(right)
    lhs = jnp.concatenate([lh, lh, lm, lh, ll, lm], axis=0).astype(bf16)
    rhs = jnp.concatenate([rh, rm, rh, rl, rh, rm], axis=0).astype(bf16)
    return lax.dot_general(lhs, rhs, (((0,), (0,)), ((), ())), preferred_element_type=f32)


def invert_half(t):
    n = t.shape[0] // 8
    lane = lax.broadcasted_iota(jnp.int32, (8, 128), 1)
    lanes = lax.broadcasted_iota(jnp.int32, (128, 128), 1)

    def step(p, tile, pivot, last):
        if not last:
            ahead = t[pl.ds(pl.multiple_of((p + 1) * 8, 8), 8), :]
            tile_next = cleared(ahead, p, pivot)
            pivot_next = pivot_panel(tile_next, p + 1)
        update = outer(jnp.where(lane < 8 * p, -tile, tile), pivot)
        t[...] = jnp.where(lanes // 8 == p, 0.0, t[...]) - update
        t[pl.ds(pl.multiple_of(p * 8, 8), 8), :] = pivot
        return None if last else (tile_next, pivot_next)

    first = t[0:8, :]
    held = lax.fori_loop(0, n - 1, lambda p, v: step(p, *v, False), (first, pivot_panel(first, 0)))
    step(n - 1, *held, True)


def invert(system, t, between=None):
    b, bt = system[0:128, 128:256], system[128:256, 0:128]
    t[...] = system[0:128, 0:128]
    invert_half(t)
    if between is not None:
        between()
    a = t[...]
    w, wt = dot(a, b), dot(bt, a)
    t[...] = system[128:256, 128:256] - dot(bt, w)
    invert_half(t)
    d = t[...]
    v, vt = dot(w, d), dot(d, wt)
    return jnp.concatenate(
        [jnp.concatenate([a + dot(v, wt), -v], axis=1), jnp.concatenate([-vt, d], axis=1)], axis=0
    )


def sweep(
    nz, nc, tensor, factor_b, factor_c, new_a, new_b, new_c,
    tensor_t, gram_c, across_b, block_b, flipped, pieces, landed, owned, ringed, chunks, grams,
    out_m, in_m, rows_a, block_a, contracted, out_b, in_b, rows_b, pieces_c, landed_c, summed_c, around_c,
    whole_c, ringed_c, system, half, sent, received,
):
    nq = nc // 2
    members, wide_a, wide_b = tensor.shape
    rank = factor_b.shape[1]
    z, c = lax.axis_index("row"), lax.axis_index("col")
    q, core = c // 2, c % 2

    barrier = pltpu.get_barrier_semaphore()

    def greet(k, carry):
        other = lax.rem(z + k, nz)
        pl.semaphore_signal(barrier, inc=1, device_id=(other, c), device_id_type=pl.DeviceIdType.MESH)
        pl.semaphore_signal(barrier, inc=1, device_id=(other, c + 1 - 2 * core), device_id_type=pl.DeviceIdType.MESH)
        return carry

    def greet_col(k, carry):
        pl.semaphore_signal(barrier, inc=1, device_id=(z, lax.rem(c + k, nc)), device_id_type=pl.DeviceIdType.MESH)
        return carry

    lax.fori_loop(1, nz, greet, 0)
    lax.fori_loop(1, nc, greet_col, 0)

    for m in range(members):
        tensor_t[m] = jnp.transpose(tensor[m])
    by_row = factor_c[...]
    gram_c[...] = lax.dot_general(
        by_row, by_row, (((0,), (0,)), ((), ())), precision=highest, preferred_element_type=f32
    )
    pl.semaphore_wait(barrier, 2 * (nz - 1) + nc - 1)

    def copy(src, dst, which, to):
        pltpu.make_async_remote_copy(
            src_ref=src, dst_ref=dst, send_sem=sent.at[which], recv_sem=received.at[which],
            device_id=to, device_id_type=pl.DeviceIdType.MESH,
        ).start()

    totals = []

    def send_z(which, src, dst, scatter=False):
        def one(k, carry):
            other = lax.rem(z + k, nz)
            copy(src.at[other] if scatter else src, dst.at[z], which, (other, c))
            return carry
        lax.fori_loop(1, nz, one, 0)
        totals.append((which, dst.at[pl.ds(0, nz - 1)]))
        dst[z] = src[z] if scatter else src[...]

    def send_zz(which, src, dst):
        me = 2 * z + core
        def one(k, carry):
            other = lax.rem(me + k, 2 * nz)
            copy(src.at[other // 2], dst.at[me], which, (other // 2, 2 * q + other % 2))
            return carry
        lax.fori_loop(1, 2 * nz, one, 0)
        totals.append((which, dst.at[pl.ds(0, 2 * nz - 1)]))
        dst[me] = src[z]

    def send_q(which, src, dst):
        def one(k, carry):
            other = lax.rem(q + k, nq)
            copy(src, dst.at[q], which, (z, 2 * other + core))
            return carry
        lax.fori_loop(1, nq, one, 0)
        totals.append((which, dst.at[pl.ds(0, nq - 1)]))
        dst[q] = src[...]

    def send_c(which, src, dst, scatter=False):
        def one(k, carry):
            other = lax.rem(c + k, nc)
            copy(src.at[other // 2] if scatter else src, dst.at[c], which, (z, other))
            return carry
        lax.fori_loop(1, nc, one, 0)
        totals.append((which, dst.at[pl.ds(0, nc - 1)]))
        dst[c] = src[q] if scatter else src[...]

    def arrived(which):
        whole = dict(totals)[which]
        pltpu.make_async_remote_copy(
            src_ref=whole, dst_ref=whole, send_sem=sent.at[which], recv_sem=received.at[which],
            device_id=(z, c), device_id_type=pl.DeviceIdType.MESH,
        ).wait_recv()

    def left(which):
        whole = dict(totals)[which]
        pltpu.make_async_remote_copy(
            src_ref=whole, dst_ref=whole, send_sem=sent.at[which], recv_sem=received.at[which],
            device_id=(z, c), device_id_type=pl.DeviceIdType.MESH,
        ).wait_send()

    def sum_of(ref):
        total = ref[0]
        for k in range(1, ref.shape[0]):
            total = total + ref[k]
        return total

    share = rank // nq
    part = share // nz

    def gram_start(turn, block, both):
        depth = block.shape[0]
        flipped[:, 0:depth] = jnp.transpose(block)
        chunk = dot(flipped[pl.ds(pl.multiple_of(q * share, 8), share), 0:depth], block)
        for k in range(nz):
            pieces[turn, k] = chunk[k * part : (k + 1) * part]
        if both:
            send_zz(3 * turn, pieces.at[turn], landed.at[turn])
        else:
            send_z(3 * turn, pieces.at[turn], landed.at[turn, pl.ds(0, nz)], True)

    def gram_middle(turn, both):
        arrived(3 * turn)
        owned[turn] = sum_of(landed.at[turn] if both else landed.at[turn, pl.ds(0, nz)])
        send_z(3 * turn + 1, owned.at[turn], ringed.at[turn])

    def gram_last(turn):
        arrived(3 * turn + 1)
        for k in range(nz):
            chunks[turn, k * part : (k + 1) * part, :] = ringed[turn, k]
        send_q(3 * turn + 2, chunks.at[turn], grams.at[turn])

    def gram_of(turn):
        arrived(3 * turn + 2)
        return grams[turn].reshape(rank, rank)

    def scales(gram, count):
        one = lax.broadcasted_iota(jnp.int32, gram.shape, 0) == lax.broadcasted_iota(jnp.int32, gram.shape, 1)
        diagonal = jnp.where(one, gram, 0.0)
        return (
            jnp.sqrt(jnp.sum(diagonal, axis=0, keepdims=True) / count + epsilon),
            jnp.sqrt(jnp.sum(diagonal, axis=1, keepdims=True) / count + epsilon),
        )

    send_q(9, factor_b, across_b.at[0])
    send_z(10, factor_b, block_b.at[0])
    arrived(9)
    gram_start(0, across_b[0].reshape(-1, rank), True)
    gram_middle(0, True)
    gram_last(0)
    arrived(10)
    products = dot(tensor[...].reshape(members * wide_a, wide_b), block_b[0].reshape(-1, rank))
    products = products.reshape(members, wide_a, rank)
    sums = products[0] * by_row[0:1]
    for m in range(1, members):
        sums = sums + products[m] * by_row[m : m + 1]
    out_m[...] = sums.reshape(nq, 8, rank)
    send_c(11, out_m, in_m, True)
    system[...] = gram_of(0) * gram_c[...]
    inverse = invert(system, half)
    arrived(11)
    rows_a[...] = dot(sum_of(in_m), inverse)

    send_q(12, rows_a, block_a)
    arrived(12)
    whole_a = block_a[...].reshape(wide_a, rank)
    gram_start(1, whole_a, False)
    contracted[...] = dot(
        tensor_t[...].reshape(members * wide_b, wide_a), whole_a
    ).reshape(members, wide_b, rank)
    gram_middle(1, False)
    sums = contracted[0] * by_row[0:1]
    for m in range(1, members):
        sums = sums + contracted[m] * by_row[m : m + 1]
    out_b[...] = sums.reshape(nz, -1, rank)
    gram_last(1)
    send_z(13, out_b, in_b, True)
    gram = gram_of(1)
    scale_a, scale_a_down = scales(gram, wide_a * nz)
    gram_a = gram / (scale_a * scale_a_down)
    system[...] = gram_a * gram_c[...]
    gram_c[...] = gram_a
    mine = rows_a[...] / scale_a
    new_a[...] = jnp.where(core == 0, mine[0:4], mine[4:8])
    inverse = invert(system, half)
    arrived(13)
    rows_b[...] = dot(sum_of(in_b) / scale_a, inverse)

    send_q(14, rows_b, across_b.at[1])
    send_z(15, rows_b, block_b.at[1])
    arrived(14)
    gram_start(2, across_b[1].reshape(-1, rank), True)
    gram_middle(2, True)
    gram_last(2)
    gram = gram_of(2)
    scale_b, scale_b_down = scales(gram, wide_b * nc)
    system[...] = gram_c[...] * (gram / (scale_b * scale_b_down))
    new_b[...] = rows_b[...] / scale_b
    arrived(15)
    next_b = block_b[1].reshape(-1, rank) / scale_b
    step = 16 // nz
    for m in range(members):
        row = jnp.sum(contracted[m] * next_b, axis=0, keepdims=True) / scale_a
        for side in range(2):
            at = 2 * m + side
            pieces_c[at // step, at % step : at % step + 1, :] = row[:, 128 * side : 128 * side + 128]
    send_z(16, pieces_c, landed_c, True)

    def between():
        arrived(16)
        summed_c[...] = sum_of(landed_c)
        send_c(17, summed_c, around_c)

    inverse = invert(system, half, between)
    arrived(17)
    whole_c[...] = sum_of(around_c)
    send_z(18, whole_c, ringed_c)
    arrived(18)
    halves = [ringed_c[at // step, at % step : at % step + 1, :] for at in range(16)]
    right_side = jnp.concatenate(
        [jnp.concatenate(halves[0::2], axis=0), jnp.concatenate(halves[1::2], axis=0)], axis=1
    )
    new_c[...] = dot(right_side, inverse)
    for which, _ in totals:
        left(which)


def solution(mesh):
    nz, nc = mesh.shape["row"], mesh.shape["col"]
    nq = nc // 2

    def on_device(tensor, factor_b, factor_c):
        members, wide_a, wide_b = tensor.shape
        deep_b, rank = factor_b.shape
        share = rank // nq
        part = share // nz
        step = 16 // nz
        memory = [
            (members, wide_b, wide_a),
            (rank, rank),
            (2, nq, deep_b, rank),
            (2, nz, deep_b, rank),
            (rank, max(nq * deep_b, wide_a)),
            (3, nz, part, rank),
            (3, 2 * nz, part, rank),
            (3, part, rank),
            (3, nz, part, rank),
            (3, share, rank),
            (3, nq, share, rank),
            (nq, 8, rank),
            (nc, 8, rank),
            (8, rank),
            (nq, 8, rank),
            (members, wide_b, rank),
            (nz, deep_b, rank),
            (nz, deep_b, rank),
            (deep_b, rank),
            (nz, step, 128),
            (nz, step, 128),
            (step, 128),
            (nc, step, 128),
            (step, 128),
            (nz, step, 128),
            (rank, rank),
            (128, 128),
        ]
        return pl.pallas_call(
            functools.partial(sweep, nz, nc),
            out_shape=(
                jax.ShapeDtypeStruct((wide_a // nc, rank), f32),
                jax.ShapeDtypeStruct((deep_b, rank), f32),
                jax.ShapeDtypeStruct((members, rank), f32),
            ),
            in_specs=[pl.BlockSpec(memory_space=pltpu.VMEM)] * 3,
            out_specs=tuple([pl.BlockSpec(memory_space=pltpu.VMEM)] * 3),
            scratch_shapes=[pltpu.VMEM(shape, f32) for shape in memory]
            + [pltpu.SemaphoreType.DMA((EXCHANGES,)), pltpu.SemaphoreType.DMA((EXCHANGES,))],
            compiler_params=pltpu.CompilerParams(
                collective_id=0, has_side_effects=True, vmem_limit_bytes=40 * 1024 * 1024
            ),
        )(tensor, factor_b, factor_c)

    return jax.shard_map(
        on_device,
        mesh=mesh,
        in_specs=(P(None, "row", "col"), P("row", "col"), P()),
        out_specs=(P(("row", "col"), None), P("row", "col"), P()),
        check_vma=False,
    )
```

time: 1860 us -> 147 us (0.08)
  waiting for transfers between devices: 1450 us -> 0 us
  blocking collectives: 187 us -> 0 us
  other arithmetic: 164 us -> 0 us
  Pallas kernels: 0 us -> 142 us
  matrix products: 22.3 us -> 0 us
    psum x3 -> x0, waiting for transfers between devices: 1350 us -> none  [the longest x1 467 us: on_device(): gram_raw_b = lax.psum(product(raw_b.T, raw_b), ('row', 'col'))]
    another operation x28 -> x0, other arithmetic: 163 us -> none  [the longest x20 103 us: solve_rows(): lower_factor = jnp.linalg.cholesky(system)]
    pallas_call x0 -> x1, Pallas kernels: none -> 142 us  [on_device(): pl.pallas_call(functools.partial(sweep, nz, nc), out_shape=(jax.ShapeDtyp...]
    psum x1 -> x0, blocking collectives: 106 us -> none  [on_device(): mttkrp_c = lax.psum(partial_c, ('row', 'col'))]
    all_gather x3 -> x0, blocking collectives: 80.9 us -> none  [the longest x1 30.7 us: on_device(): block_b = lax.all_gather(factor_b, 'row', axis=0, tiled=True)]
    unnamed x6 -> x0, waiting for transfers between devices: 69.5 us -> none
    reduce_scatter x1 -> x0, waiting for transfers between devices: 25.8 us -> none  [on_device(): lax.psum_scatter(partial_b, 'row', scatter_dimension=0, tiled=True)]
  transfers between devices with their start and end apart: 5 -> 0, of which waited for: 5 -> 0; matrix products, arithmetic and copies ran while one was open for 5% -> 0% of each run, Pallas kernels for 0% -> 0%
where the time goes in v1:
time: 147 us
  Pallas kernels  142 us (97%)
  local copies, waits for them, and re-layouts  4.43 us (3%)
    pallas_call x1, Pallas kernels, on_device(): pl.pallas_call(functools.partial(sweep, nz, nc), out_shape=(jax.ShapeDtyp...  142 us
    unnamed x9, local copies, waits for them, and re-layouts  4.43 us

profile of v1, /device:TPU:1, one launch (start us, length us, event | category | flops | bytes accessed | tf_op | source)
XLA Modules:
  0.0 147.0 jit_solution(8426710699727625555)
XLA Ops:
  0.6 0.0 copy-start
  0.6 1.2 copy-done
  1.9 0.0 copy-start.1
  1.9 0.7 copy-done.1
  2.6 0.0 copy-start.2
  2.6 0.7 copy-done.2
  3.3 141.9 %shard_map.58 = (f32[4,256]{1,0:T(4,128)S(1)}, f32[16,256]{1,0:T(8,128)S(1)}, f32[8,256]{1,0:T(8,128)S(1)}) custom-call(f32[8,128,256]{2,1,0:T(8,128)S(1)} %copy-done, f32[16,256]{1,0:T(8,128)S(1)} %copy-done.1, f32[8,256]{1,0:T(8,128)S(1)} %copy-done.2), custom_call_target="tpu_custom_call" | custom-call | tf_op jit(solution)/shard_map/pallas_call | solution.py:365
  145.2 0.6 copy.9
  145.8 0.6 copy.10
  146.4 0.6 copy.11
Async XLA Ops:
  0.6 1.2 copy-start
  1.9 0.7 copy-start.1
  2.6 0.7 copy-start.2

commit v2 on v1

v2 whole, which is shorter than its diff:
```python
import functools

import jax
import jax.numpy as jnp
from jax import lax
from jax.experimental import pallas as pl
from jax.experimental.pallas import tpu as pltpu
from jax.sharding import PartitionSpec as P

f32 = jnp.float32
bf16 = jnp.bfloat16
highest = lax.Precision.HIGHEST
epsilon = 1e-06
EXCHANGES = 20
MESH = pl.DeviceIdType.MESH


def dot(left, right):
    return jnp.dot(left, right, precision=highest, preferred_element_type=f32)


def lane_of(tile, index):
    return jnp.take_along_axis(tile, jnp.full(tile.shape, index, jnp.int32), axis=1)


def row_of(tile, k):
    return jnp.broadcast_to(tile[k : k + 1], tile.shape)


def added(parts):
    while len(parts) > 1:
        parts = [a + b for a, b in zip(parts[::2], parts[1::2])] + parts[len(parts) & ~1 :]
    return parts[0]


def pivot_panel(tile, p):
    lane = lax.broadcasted_iota(jnp.int32, (8, 128), 1)
    sub = lax.broadcasted_iota(jnp.int32, (8, 128), 0)
    d = [lane_of(tile, p * 8 + k) for k in range(8)]
    for j in range(8):
        here = sub == j
        c = jnp.where(here, -1.0, d[j]) * (1.0 / row_of(d[j], j))
        d = [-c if k == j else jnp.where(here, 0.0, d[k]) - c * row_of(d[k], j) for k in range(8)]
    rows = jnp.where(lane // 8 == p, jnp.where(lane % 8 == sub, 1.0, 0.0), tile)
    return added([d[k] * row_of(rows, k) for k in range(8)])


def cleared(tile, p, pivot):
    lane = lax.broadcasted_iota(jnp.int32, (8, 128), 1)
    return jnp.where(lane // 8 == p, 0.0, tile) - added(
        [lane_of(tile, p * 8 + k) * row_of(pivot, k) for k in range(8)]
    )


def thirds(x):
    high = x.astype(bf16).astype(f32)
    rest = x - high
    middle = rest.astype(bf16).astype(f32)
    return high, middle, rest - middle


def outer(left, right):
    lh, lm, ll = thirds(left)
    rh, rm, rl = thirds(right)
    lhs = jnp.concatenate([lh, lh, lm, lh, ll, lm], axis=0).astype(bf16)
    rhs = jnp.concatenate([rh, rm, rh, rl, rh, rm], axis=0).astype(bf16)
    return lax.dot_general(lhs, rhs, (((0,), (0,)), ((), ())), preferred_element_type=f32)


def invert_half(t):
    n = t.shape[0] // 8
    lane = lax.broadcasted_iota(jnp.int32, (8, 128), 1)
    lanes = lax.broadcasted_iota(jnp.int32, (128, 128), 1)

    def step(p, tile, pivot, last):
        if not last:
            ahead = t[pl.ds(pl.multiple_of((p + 1) * 8, 8), 8), :]
            tile_next = cleared(ahead, p, pivot)
            pivot_next = pivot_panel(tile_next, p + 1)
        update = outer(jnp.where(lane < 8 * p, -tile, tile), pivot)
        t[...] = jnp.where(lanes // 8 == p, 0.0, t[...]) - update
        t[pl.ds(pl.multiple_of(p * 8, 8), 8), :] = pivot
        return None if last else (tile_next, pivot_next)

    first = t[0:8, :]
    held = lax.fori_loop(0, n - 1, lambda p, v: step(p, *v, False), (first, pivot_panel(first, 0)))
    step(n - 1, *held, True)


def invert(system, t, between=None):
    b, bt = system[0:128, 128:256], system[128:256, 0:128]
    t[...] = system[0:128, 0:128]
    invert_half(t)
    if between is not None:
        between()
    a = t[...]
    w, wt = dot(a, b), dot(bt, a)
    t[...] = system[128:256, 128:256] - dot(bt, w)
    invert_half(t)
    d = t[...]
    v, vt = dot(w, d), dot(d, wt)
    return jnp.concatenate(
        [jnp.concatenate([a + dot(v, wt), -v], axis=1), jnp.concatenate([-vt, d], axis=1)], axis=0
    )


def dot_first(left, right):
    return lax.dot_general(
        left, right, (((0,), (0,)), ((), ())), precision=highest, preferred_element_type=f32
    )


def sweep(
    nz, nc, tensor_in, factor_b_in, factor_c_in, new_a, new_b, new_c,
    tensor, factor_b, factor_c, tensor_t, gram_c, block_b, partial, landed, owned, grams,
    out_m, in_m, rows_m, ring_m, block_m, contracted, out_b, near_b, part_b, far_b, rows_b,
    out_c, in_c, half_c, ring_c, side_c, system, half, sent, received, loaded,
):
    nq, nk = nc // 2, nz // 4
    z, c = lax.axis_index("row"), lax.axis_index("col")
    q, core = c // 2, c % 2
    class_z, place_z = z % 4, z // 4

    loads = [
        pltpu.make_async_copy(src, dst, loaded.at[i])
        for i, (src, dst) in enumerate(((factor_b_in, factor_b), (tensor_in, tensor), (factor_c_in, factor_c)))
    ]
    for load in loads:
        load.start()

    barrier = pltpu.get_barrier_semaphore()

    def greet_z(k, carry):
        pl.semaphore_signal(barrier, inc=1, device_id=(lax.rem(z + k, nz), c), device_id_type=MESH)
        return carry

    def greet_c(k, carry):
        pl.semaphore_signal(barrier, inc=1, device_id=(z, lax.rem(c + k, nc)), device_id_type=MESH)
        return carry

    lax.fori_loop(1, nz, greet_z, 0)
    lax.fori_loop(1, nc, greet_c, 0)

    for load in loads:
        load.wait()
    members, wide_a, wide_b = tensor.shape
    rank = factor_b.shape[1]
    for m in range(members):
        tensor_t[m] = jnp.transpose(tensor[m])
    by_row = factor_c[...]
    gram_c[...] = dot_first(by_row, by_row)
    pl.semaphore_wait(barrier, nz - 1 + nc - 1)

    def copy(which, src, dst, to):
        return pltpu.make_async_remote_copy(
            src_ref=src, dst_ref=dst, send_sem=sent.at[which], recv_sem=received.at[which],
            device_id=to, device_id_type=MESH,
        )

    totals = {}

    def over(which, whole):
        totals[which] = whole

    def arrived(which):
        if which in totals:
            copy(which, totals[which], totals[which], (z, c)).wait_recv()

    def send_all_z(which, src, dst):
        def one(k, carry):
            copy(which, src, dst.at[z], (lax.rem(z + k, nz), c)).start()
            return carry
        lax.fori_loop(1, nz, one, 0)
        over(which, dst.at[pl.ds(0, nz - 1)])
        dst[z] = src[...]

    def send_q(which, src, dst, scatter=False):
        def one(k, carry):
            other = lax.rem(q + k, nq)
            copy(which, src.at[2 * other + core] if scatter else src, dst.at[q], (z, 2 * other + core)).start()
            return carry
        lax.fori_loop(1, nq, one, 0)
        if nq > 1:
            over(which, dst.at[pl.ds(0, nq - 1)])
        dst[q] = src[c] if scatter else src[...]

    def send_c(which, src, dst, pick=None):
        def one(k, carry):
            other = lax.rem(c + k, nc)
            copy(which, src.at[pick(other)] if pick else src, dst.at[c], (z, other)).start()
            return carry
        lax.fori_loop(1, nc, one, 0)
        over(which, dst.at[pl.ds(0, nc - 1)])
        dst[c] = src[pick(c)] if pick else src[...]

    def sum_of(ref):
        total = ref[0]
        for k in range(1, ref.shape[0]):
            total = total + ref[k]
        return total

    def gather_far(which, src, dst):
        for k in range(1, nk):
            copy(which, src, dst.at[class_z, place_z], (lax.rem(z + 4 * k, nz), c)).start()
        if nk > 1:
            over(which, dst.at[0, pl.ds(0, nk - 1)])
        dst[class_z, place_z] = src[...]

    def gather_near(which, dst):
        for k in (1, nz - 1, 2):
            copy(which, dst.at[class_z], dst.at[class_z], (lax.rem(z + k, nz), c)).start()
        over(which, dst.at[pl.ds(0, 3)])

    def gathered(ref):
        return jnp.concatenate([ref[k % 4, k // 4] for k in range(nz)], axis=0)

    def scatter_near(which, src, dst):
        for slot, k in enumerate((1, nz - 1, 2)):
            copy(which, src.at[lax.rem(z + k, 4)], dst.at[slot], (lax.rem(z + k, nz), c)).start()
        over(which, dst.at[pl.ds(0, 3)])

    def scatter_far(which, src, dst):
        for k in range(1, nk):
            other = lax.rem(z + 4 * k, nz)
            copy(which, src.at[other // 4], dst.at[k - 1], (other, c)).start()
        if nk > 1:
            over(which, dst.at[pl.ds(0, nk - 1)])

    part = rank // nc

    def gram_start(turn, block, both):
        partial[turn] = dot_first(block, block).reshape(nc, part, rank)
        if both:
            send_c(3 * turn, partial.at[turn], landed.at[turn], lambda other: other)
        else:
            send_q(3 * turn, partial.at[turn], landed.at[turn, pl.ds(0, nq)], True)

    def gram_middle(turn, both):
        arrived(3 * turn)
        owned[turn] = sum_of(landed.at[turn] if both else landed.at[turn, pl.ds(0, nq)])
        send_c(3 * turn + 1, owned.at[turn], grams.at[turn])

    def gram_of(turn):
        arrived(3 * turn + 1)
        return grams[turn].reshape(rank, rank)

    def scales(gram, count):
        one = lax.broadcasted_iota(jnp.int32, gram.shape, 0) == lax.broadcasted_iota(jnp.int32, gram.shape, 1)
        diagonal = jnp.where(one, gram, 0.0)
        return (
            jnp.sqrt(jnp.sum(diagonal, axis=0, keepdims=True) / count + epsilon),
            jnp.sqrt(jnp.sum(diagonal, axis=1, keepdims=True) / count + epsilon),
        )

    gather_far(2, factor_b, block_b.at[0])
    arrived(2)
    gather_near(5, block_b.at[0])
    arrived(5)
    whole_b = gathered(block_b.at[0])
    gram_start(0, whole_b, True)
    products = dot(tensor[...].reshape(members * wide_a, wide_b), whole_b).reshape(members, wide_a, rank)
    sums = products[0] * by_row[0:1]
    for m in range(1, members):
        sums = sums + products[m] * by_row[m : m + 1]
    out_m[...] = sums.reshape(nq, 8, rank)
    send_c(9, out_m, in_m, lambda other: other // 2)
    gram_middle(0, True)
    arrived(9)
    rows_m[...] = sum_of(in_m)
    send_all_z(10, rows_m, ring_m)
    send_q(11, rows_m, block_m)
    system[...] = gram_of(0) * gram_c[...]
    inverse = invert(system, half)

    arrived(10)
    gram_start(1, dot(ring_m[...].reshape(nz * 8, rank), inverse), False)
    arrived(11)
    whole_a = dot(block_m[...].reshape(wide_a, rank), inverse)
    contracted[...] = dot(
        tensor_t[...].reshape(members * wide_b, wide_a), whole_a
    ).reshape(members, wide_b, rank)
    sums = contracted[0] * by_row[0:1]
    for m in range(1, members):
        sums = sums + contracted[m] * by_row[m : m + 1]
    sums = sums.reshape(nz, -1, rank)
    for k in range(nz):
        out_b[k % 4, k // 4] = sums[k]
    scatter_near(12, out_b, near_b)
    gram_middle(1, False)
    raw_a = dot(rows_m[...], inverse)
    arrived(12)
    part_b[...] = (out_b[class_z] + near_b[0]) + (near_b[1] + near_b[2])
    scatter_far(13, part_b, far_b)
    gram = gram_of(1)
    scale_a, scale_a_down = scales(gram, wide_a * nz)
    gram_a = gram / (scale_a * scale_a_down)
    system[...] = gram_a * gram_c[...]
    gram_c[...] = gram_a

    def rows_b_known():
        raw_a_scaled = raw_a / scale_a
        new_a[...] = jnp.where(core == 0, raw_a_scaled[0:4], raw_a_scaled[4:8])
        arrived(13)
        total = part_b[place_z]
        for k in range(nk - 1):
            total = total + far_b[k]
        rows_b[...] = total / scale_a
        gather_far(14, rows_b, block_b.at[1])

    inverse = invert(system, half, rows_b_known)
    arrived(14)
    gather_near(15, block_b.at[1])
    for m in range(members):
        contracted[m] = contracted[m] / scale_a
    arrived(15)

    raw_b = dot(gathered(block_b.at[1]), inverse)
    gram_start(2, raw_b, True)
    sums = jnp.concatenate(
        [jnp.sum(contracted[m] * raw_b, axis=0, keepdims=True) for m in range(members)], axis=0
    )
    out_c[0] = sums[:, 0:128]
    out_c[1] = sums[:, 128:256]
    send_c(16, out_c, in_c, lambda other: other % 2)
    raw_b_own = dot(rows_b[...], inverse)
    gram_middle(2, True)
    arrived(16)
    half_c[...] = sum_of(in_c)
    send_all_z(17, half_c, ring_c)
    gram = gram_of(2)
    scale_b, scale_b_down = scales(gram, wide_b * nc)
    system[...] = gram_c[...] * (gram / (scale_b * scale_b_down))
    new_b[...] = raw_b_own / scale_b

    def half_known():
        arrived(17)
        side_c[core] = sum_of(ring_c)
        copy(18, side_c.at[core], side_c.at[core], (z, c + 1 - 2 * core)).start()
        over(18, side_c.at[0])

    inverse = invert(system, half, half_known)
    arrived(18)
    new_c[...] = dot(jnp.concatenate([side_c[0], side_c[1]], axis=1) / scale_b, inverse)
    for which, whole in totals.items():
        copy(which, whole, whole, (z, c)).wait_send()


def solution(mesh):
    nz, nc = mesh.shape["row"], mesh.shape["col"]
    nq, nk = nc // 2, nz // 4

    def on_device(tensor, factor_b, factor_c):
        members, wide_a, wide_b = tensor.shape
        deep_b, rank = factor_b.shape
        part = rank // nc
        memory = [
            tensor.shape,
            factor_b.shape,
            factor_c.shape,
            (members, wide_b, wide_a),
            (rank, rank),
            (2, 4, nk, deep_b, rank),
            (3, nc, part, rank),
            (3, nc, part, rank),
            (3, part, rank),
            (3, nc, part, rank),
            (nq, 8, rank),
            (nc, 8, rank),
            (8, rank),
            (nz, 8, rank),
            (nq, 8, rank),
            (members, wide_b, rank),
            (4, nk, deep_b, rank),
            (3, nk, deep_b, rank),
            (nk, deep_b, rank),
            (max(nk - 1, 1), deep_b, rank),
            (deep_b, rank),
            (2, members, 128),
            (nc, members, 128),
            (members, 128),
            (nz, members, 128),
            (2, members, 128),
            (rank, rank),
            (128, 128),
        ]
        return pl.pallas_call(
            functools.partial(sweep, nz, nc),
            out_shape=(
                jax.ShapeDtypeStruct((wide_a // nc, rank), f32),
                jax.ShapeDtypeStruct((deep_b, rank), f32),
                jax.ShapeDtypeStruct((members, rank), f32),
            ),
            in_specs=[pl.BlockSpec(memory_space=pl.ANY)] * 3,
            out_specs=tuple([pl.BlockSpec(memory_space=pltpu.VMEM)] * 3),
            scratch_shapes=[pltpu.VMEM(shape, f32) for shape in memory]
            + [pltpu.SemaphoreType.DMA((EXCHANGES,)), pltpu.SemaphoreType.DMA((EXCHANGES,))]
            + [pltpu.SemaphoreType.DMA((3,))],
            compiler_params=pltpu.CompilerParams(
                collective_id=0, has_side_effects=True, vmem_limit_bytes=40 * 1024 * 1024
            ),
        )(tensor, factor_b, factor_c)

    return jax.shard_map(
        on_device,
        mesh=mesh,
        in_specs=(P(None, "row", "col"), P("row", "col"), P()),
        out_specs=(P(("row", "col"), None), P("row", "col"), P()),
        check_vma=False,
    )
```

time: 147 us -> 114 us (0.78)
  Pallas kernels: 142 us -> 109 us
    pallas_call x1, Pallas kernels: 142 us -> 109 us  [on_device(): pl.pallas_call(functools.partial(sweep, nz, nc), out_shape=(jax.ShapeDtyp...]
where the time goes in v2:
time: 114 us
  Pallas kernels  109 us (96%)
  local copies, waits for them, and re-layouts  4.43 us (4%)
    pallas_call x1, Pallas kernels, on_device(): pl.pallas_call(functools.partial(sweep, nz, nc), out_shape=(jax.ShapeDtyp...  109 us
    unnamed x9, local copies, waits for them, and re-layouts  4.43 us

profile of v2, /device:TPU:1, one launch (start us, length us, event | category | flops | bytes accessed | tf_op | source)
XLA Modules:
  0.0 113.7 jit_solution(1778471211412820693)
XLA Ops:
  0.6 0.0 copy-start
  0.6 1.2 %copy-done = f32[8,128,256]{2,1,0:T(8,128)S(1)} copy-done((f32[8,128,256]{2,1,0:T(8,128)S(1)}, f32[8,128,256]{2,1,0:T(8,128)}, u32[]{:S(2)}) %copy-start) | copy-done | bytes 1048600
  1.9 0.0 copy-start.1
  1.9 0.7 copy-done.1
  2.6 0.0 copy-start.2
  2.6 0.7 copy-done.2
  3.3 108.6 %shard_map.58 = (f32[4,256]{1,0:T(4,128)S(1)}, f32[16,256]{1,0:T(8,128)S(1)}, f32[8,256]{1,0:T(8,128)S(1)}) custom-call(f32[8,128,256]{2,1,0:T(8,128)S(1)} %copy-done, f32[16,256]{1,0:T(8,128)S(1)} %copy-done.1, f32[8,256]{1,0:T(8,128)S(1)} %copy-done.2), custom_call_target="tpu_custom_call" | custom-call | tf_op jit(solution)/shard_map/pallas_call | solution.py:386
  111.9 0.6 copy.9
  112.5 0.6 copy.10
  113.1 0.6 copy.11
Async XLA Ops:
  0.6 1.2 %copy-start = (f32[8,128,256]{2,1,0:T(8,128)S(1)}, f32[8,128,256]{2,1,0:T(8,128)}, u32[]{:S(2)}) copy-start(f32[8,128,256]{2,1,0:T(8,128)} %tensor_in.1) | copy-start | bytes 3145732
  1.9 0.7 copy-start.1
  2.6 0.7 copy-start.2

commit v3 on v2

--- a/solution.py
+++ b/solution.py
@@ -11,7 +11,7 @@
 bf16 = jnp.bfloat16
 highest = lax.Precision.HIGHEST
 epsilon = 1e-06
-EXCHANGES = 20
+EXCHANGES = 32
 MESH = pl.DeviceIdType.MESH
 
 
@@ -39,8 +39,10 @@
     d = [lane_of(tile, p * 8 + k) for k in range(8)]
     for j in range(8):
         here = sub == j
-        c = jnp.where(here, -1.0, d[j]) * (1.0 / row_of(d[j], j))
-        d = [-c if k == j else jnp.where(here, 0.0, d[k]) - c * row_of(d[k], j) for k in range(8)]
+        c = jnp.where(here, -1.0, d[j])
+        products = [None if k == j else c * row_of(d[k], j) for k in range(8)]
+        r = 1.0 / row_of(d[j], j)
+        d = [-c * r if k == j else jnp.where(here, 0.0, d[k]) - products[k] * r for k in range(8)]
     rows = jnp.where(lane // 8 == p, jnp.where(lane % 8 == sub, 1.0, 0.0), tile)
     return added([d[k] * row_of(rows, k) for k in range(8)])
 
@@ -83,7 +85,9 @@
         return None if last else (tile_next, pivot_next)
 
     first = t[0:8, :]
-    held = lax.fori_loop(0, n - 1, lambda p, v: step(p, *v, False), (first, pivot_panel(first, 0)))
+    held = lax.fori_loop(
+        0, n - 1, lambda p, v: step(p, *v, False), (first, pivot_panel(first, 0)), unroll=3
+    )
     step(n - 1, *held, True)
 
 
@@ -146,7 +150,7 @@
     members, wide_a, wide_b = tensor.shape
     rank = factor_b.shape[1]
     for m in range(members):
-        tensor_t[m] = jnp.transpose(tensor[m])
+        tensor_t[:, m * wide_a : (m + 1) * wide_a] = jnp.transpose(tensor[m])
     by_row = factor_c[...]
     gram_c[...] = dot_first(by_row, by_row)
     pl.semaphore_wait(barrier, nz - 1 + nc - 1)
@@ -159,6 +163,9 @@
 
     totals = {}
 
+    def hops(k):
+        return -(min(k % 4, 4 - k % 4) + min(k // 4, 4 - k // 4))
+
     def over(which, whole):
         totals[which] = whole
 
@@ -167,29 +174,23 @@
             copy(which, totals[which], totals[which], (z, c)).wait_recv()
 
     def send_all_z(which, src, dst):
-        def one(k, carry):
+        for k in sorted(range(1, nz), key=lambda k: -min(k, nz - k)):
             copy(which, src, dst.at[z], (lax.rem(z + k, nz), c)).start()
-            return carry
-        lax.fori_loop(1, nz, one, 0)
         over(which, dst.at[pl.ds(0, nz - 1)])
         dst[z] = src[...]
 
     def send_q(which, src, dst, scatter=False):
-        def one(k, carry):
+        for k in sorted(range(1, nq), key=hops):
             other = lax.rem(q + k, nq)
             copy(which, src.at[2 * other + core] if scatter else src, dst.at[q], (z, 2 * other + core)).start()
-            return carry
-        lax.fori_loop(1, nq, one, 0)
         if nq > 1:
             over(which, dst.at[pl.ds(0, nq - 1)])
         dst[q] = src[c] if scatter else src[...]
 
     def send_c(which, src, dst, pick=None):
-        def one(k, carry):
+        for k in sorted(range(1, nc), key=lambda k: hops(k // 2)):
             other = lax.rem(c + k, nc)
             copy(which, src.at[pick(other)] if pick else src, dst.at[c], (z, other)).start()
-            return carry
-        lax.fori_loop(1, nc, one, 0)
         over(which, dst.at[pl.ds(0, nc - 1)])
         dst[c] = src[pick(c)] if pick else src[...]
 
@@ -199,17 +200,30 @@
             total = total + ref[k]
         return total
 
-    def gather_far(which, src, dst):
-        for k in range(1, nk):
-            copy(which, src, dst.at[class_z, place_z], (lax.rem(z + 4 * k, nz), c)).start()
-        if nk > 1:
-            over(which, dst.at[0, pl.ds(0, nk - 1)])
+    far = sorted(range(1, nk), key=lambda k: -min(k, nk - k))
+
+    def to_near(which, block):
+        for k in (2, 1, nz - 1):
+            copy(which, block, block, (lax.rem(z + k, nz), c)).start()
+
+    def gather_start(which, src, dst):
+        for k in far:
+            copy(which + k, src, dst.at[class_z, place_z], (lax.rem(z + 4 * k, nz), c)).start()
+            over(which + k, dst.at[0, 0])
         dst[class_z, place_z] = src[...]
-
-    def gather_near(which, dst):
-        for k in (1, nz - 1, 2):
-            copy(which, dst.at[class_z], dst.at[class_z], (lax.rem(z + k, nz), c)).start()
-        over(which, dst.at[pl.ds(0, 3)])
+        to_near(which, dst.at[class_z, place_z])
+        over(which, dst.at[pl.ds(0, 3), 0])
+
+    def gather_on(which, dst):
+        for k in reversed(far):
+            arrived(which + k)
+            to_near(which + nk - 1 + k, dst.at[class_z, lax.rem(place_z + nk - k, nk)])
+            over(which + nk - 1 + k, dst.at[pl.ds(0, 3), 0])
+
+    def gather_end(which):
+        arrived(which)
+        for k in reversed(far):
+            arrived(which + nk - 1 + k)
 
     def gathered(ref):
         return jnp.concatenate([ref[k % 4, k // 4] for k in range(nz)], axis=0)
@@ -252,10 +266,9 @@
             jnp.sqrt(jnp.sum(diagonal, axis=1, keepdims=True) / count + epsilon),
         )
 
-    gather_far(2, factor_b, block_b.at[0])
-    arrived(2)
-    gather_near(5, block_b.at[0])
-    arrived(5)
+    gather_start(18, factor_b, block_b.at[0])
+    gather_on(18, block_b.at[0])
+    gather_end(18)
     whole_b = gathered(block_b.at[0])
     gram_start(0, whole_b, True)
     products = dot(tensor[...].reshape(members * wide_a, wide_b), whole_b).reshape(members, wide_a, rank)
@@ -272,47 +285,42 @@
     system[...] = gram_of(0) * gram_c[...]
     inverse = invert(system, half)
 
-    arrived(10)
-    gram_start(1, dot(ring_m[...].reshape(nz * 8, rank), inverse), False)
     arrived(11)
     whole_a = dot(block_m[...].reshape(wide_a, rank), inverse)
-    contracted[...] = dot(
-        tensor_t[...].reshape(members * wide_b, wide_a), whole_a
-    ).reshape(members, wide_b, rank)
-    sums = contracted[0] * by_row[0:1]
-    for m in range(1, members):
-        sums = sums + contracted[m] * by_row[m : m + 1]
-    sums = sums.reshape(nz, -1, rank)
+    weighted = jnp.concatenate([whole_a * by_row[m : m + 1] for m in range(members)], axis=0)
+    sums = dot(tensor_t[...], weighted).reshape(nz, -1, rank)
     for k in range(nz):
         out_b[k % 4, k // 4] = sums[k]
     scatter_near(12, out_b, near_b)
-    gram_middle(1, False)
+    arrived(10)
+    gram_start(1, dot(ring_m[...].reshape(nz * 8, rank), inverse), False)
+    for m in range(members):
+        contracted[m] = dot(tensor_t[:, m * wide_a : (m + 1) * wide_a], whole_a)
     raw_a = dot(rows_m[...], inverse)
     arrived(12)
     part_b[...] = (out_b[class_z] + near_b[0]) + (near_b[1] + near_b[2])
     scatter_far(13, part_b, far_b)
+    gram_middle(1, False)
     gram = gram_of(1)
     scale_a, scale_a_down = scales(gram, wide_a * nz)
     gram_a = gram / (scale_a * scale_a_down)
     system[...] = gram_a * gram_c[...]
     gram_c[...] = gram_a
-
-    def rows_b_known():
-        raw_a_scaled = raw_a / scale_a
-        new_a[...] = jnp.where(core == 0, raw_a_scaled[0:4], raw_a_scaled[4:8])
-        arrived(13)
-        total = part_b[place_z]
-        for k in range(nk - 1):
-            total = total + far_b[k]
-        rows_b[...] = total / scale_a
-        gather_far(14, rows_b, block_b.at[1])
-
-    inverse = invert(system, half, rows_b_known)
-    arrived(14)
-    gather_near(15, block_b.at[1])
+    arrived(13)
+    total = part_b[place_z]
+    for k in range(nk - 1):
+        total = total + far_b[k]
+    rows_b[...] = total / scale_a
+    gather_start(25, rows_b, block_b.at[1])
+    inverse = invert(system, half)
+    gather_on(25, block_b.at[1])
+    raw_a_scaled = raw_a / scale_a
+    new_a[...] = jnp.where(core == 0, raw_a_scaled[0:4], raw_a_scaled[4:8])
+    per_scale_a = 1.0 / scale_a
     for m in range(members):
-        contracted[m] = contracted[m] / scale_a
-    arrived(15)
+        contracted[m] = contracted[m] * per_scale_a
+    raw_b_own = dot(rows_b[...], inverse)
+    gather_end(25)
 
     raw_b = dot(gathered(block_b.at[1]), inverse)
     gram_start(2, raw_b, True)
@@ -322,7 +330,6 @@
     out_c[0] = sums[:, 0:128]
     out_c[1] = sums[:, 128:256]
     send_c(16, out_c, in_c, lambda other: other % 2)
-    raw_b_own = dot(rows_b[...], inverse)
     gram_middle(2, True)
     arrived(16)
     half_c[...] = sum_of(in_c)
@@ -335,11 +342,11 @@
     def half_known():
         arrived(17)
         side_c[core] = sum_of(ring_c)
-        copy(18, side_c.at[core], side_c.at[core], (z, c + 1 - 2 * core)).start()
-        over(18, side_c.at[0])
+        copy(15, side_c.at[core], side_c.at[core], (z, c + 1 - 2 * core)).start()
+        over(15, side_c.at[0])
 
     inverse = invert(system, half, half_known)
-    arrived(18)
+    arrived(15)
     new_c[...] = dot(jnp.concatenate([side_c[0], side_c[1]], axis=1) / scale_b, inverse)
     for which, whole in totals.items():
         copy(which, whole, whole, (z, c)).wait_send()
@@ -357,7 +364,7 @@
             tensor.shape,
             factor_b.shape,
             factor_c.shape,
-            (members, wide_b, wide_a),
+            (wide_b, members * wide_a),
             (rank, rank),
             (2, 4, nk, deep_b, rank),
             (3, nc, part, rank),
@@ -390,7 +397,7 @@
                 jax.ShapeDtypeStruct((deep_b, rank), f32),
                 jax.ShapeDtypeStruct((members, rank), f32),
             ),
-            in_specs=[pl.BlockSpec(memory_space=pl.ANY)] * 3,
+            in_specs=[pl.BlockSpec(memory_space=pltpu.HBM)] * 3,
             out_specs=tuple([pl.BlockSpec(memory_space=pltpu.VMEM)] * 3),
             scratch_shapes=[pltpu.VMEM(shape, f32) for shape in memory]
             + [pltpu.SemaphoreType.DMA((EXCHANGES,)), pltpu.SemaphoreType.DMA((EXCHANGES,))]

time: 114 us -> 105 us (0.921)
  Pallas kernels: 109 us -> 99.9 us
    pallas_call x1, Pallas kernels: 109 us -> 99.9 us  [on_device(): pl.pallas_call(functools.partial(sweep, nz, nc), out_shape=(jax.ShapeDtyp...]
where the time goes in v3:
time: 105 us
  Pallas kernels  99.9 us (95%)
  local copies, waits for them, and re-layouts  4.43 us (4%)
    pallas_call x1, Pallas kernels, on_device(): pl.pallas_call(functools.partial(sweep, nz, nc), out_shape=(jax.ShapeDtyp...  99.9 us
    unnamed x9, local copies, waits for them, and re-layouts  4.43 us

profile of v3, /device:TPU:1, one launch (start us, length us, event | category | flops | bytes accessed | tf_op | source)
XLA Modules:
  0.0 105.0 jit_solution(15613623253040463531)
XLA Ops:
  0.6 0.0 copy-start
  0.6 1.2 %copy-done = f32[8,128,256]{2,1,0:T(8,128)S(1)} copy-done((f32[8,128,256]{2,1,0:T(8,128)S(1)}, f32[8,128,256]{2,1,0:T(8,128)}, u32[]{:S(2)}) %copy-start) | copy-done | bytes 1048600
  1.9 0.0 copy-start.1
  1.9 0.7 copy-done.1
  2.6 0.0 copy-start.2
  2.6 0.7 copy-done.2
  3.3 99.9 %shard_map.58 = (f32[4,256]{1,0:T(4,128)S(1)}, f32[16,256]{1,0:T(8,128)S(1)}, f32[8,256]{1,0:T(8,128)S(1)}) custom-call(f32[8,128,256]{2,1,0:T(8,128)S(1)} %copy-done, f32[16,256]{1,0:T(8,128)S(1)} %copy-done.1, f32[8,256]{1,0:T(8,128)S(1)} %copy-done.2), custom_call_target="tpu_custom_call" | custom-call | tf_op jit(solution)/shard_map/pallas_call | solution.py:393
  103.2 0.6 copy.9
  103.8 0.6 copy.10
  104.4 0.6 copy.11
Async XLA Ops:
  0.6 1.2 %copy-start = (f32[8,128,256]{2,1,0:T(8,128)S(1)}, f32[8,128,256]{2,1,0:T(8,128)}, u32[]{:S(2)}) copy-start(f32[8,128,256]{2,1,0:T(8,128)} %tensor_in.1) | copy-start | bytes 3145732
  1.9 0.7 copy-start.1
  2.6 0.7 copy-start.2

commit v4 on v3

v4 whole, which is shorter than its diff:
```python
import functools

import jax
import jax.numpy as jnp
from jax import lax
from jax.experimental import pallas as pl
from jax.experimental.pallas import tpu as pltpu
from jax.sharding import PartitionSpec as P

f32 = jnp.float32
bf16 = jnp.bfloat16
highest = lax.Precision.HIGHEST
epsilon = 1e-06
EXCHANGES = 36
MESH = pl.DeviceIdType.MESH


def dot(left, right):
    return jnp.dot(left, right, precision=highest, preferred_element_type=f32)


def lane_of(tile, index):
    return jnp.take_along_axis(tile, jnp.full(tile.shape, index, jnp.int32), axis=1)


def row_of(tile, k):
    return jnp.broadcast_to(tile[k : k + 1], tile.shape)


def added(parts):
    while len(parts) > 1:
        parts = [a + b for a, b in zip(parts[::2], parts[1::2])] + parts[len(parts) & ~1 :]
    return parts[0]


def pivot_panel(tile, p):
    lane = lax.broadcasted_iota(jnp.int32, (8, 128), 1)
    sub = lax.broadcasted_iota(jnp.int32, (8, 128), 0)
    d = [lane_of(tile, p * 8 + k) for k in range(8)]
    for j in range(8):
        here = sub == j
        c = jnp.where(here, -1.0, d[j])
        products = [None if k == j else c * row_of(d[k], j) for k in range(8)]
        r = 1.0 / row_of(d[j], j)
        d = [-c * r if k == j else jnp.where(here, 0.0, d[k]) - products[k] * r for k in range(8)]
    rows = jnp.where(lane // 8 == p, jnp.where(lane % 8 == sub, 1.0, 0.0), tile)
    return added([d[k] * row_of(rows, k) for k in range(8)])


def cleared(tile, p, pivot):
    lane = lax.broadcasted_iota(jnp.int32, (8, 128), 1)
    return jnp.where(lane // 8 == p, 0.0, tile) - added(
        [lane_of(tile, p * 8 + k) * row_of(pivot, k) for k in range(8)]
    )


def thirds(x):
    high = x.astype(bf16).astype(f32)
    rest = x - high
    middle = rest.astype(bf16).astype(f32)
    return high, middle, rest - middle


def outer(left, right):
    lh, lm, ll = thirds(left)
    rh, rm, rl = thirds(right)
    lhs = jnp.concatenate([lh, lh, lm, lh, ll, lm], axis=0).astype(bf16)
    rhs = jnp.concatenate([rh, rm, rh, rl, rh, rm], axis=0).astype(bf16)
    return lax.dot_general(lhs, rhs, (((0,), (0,)), ((), ())), preferred_element_type=f32)


def invert_half(t):
    n = t.shape[0] // 8
    lane = lax.broadcasted_iota(jnp.int32, (8, 128), 1)
    lanes = lax.broadcasted_iota(jnp.int32, (128, 128), 1)

    def step(p, tile, pivot, last):
        if not last:
            ahead = t[pl.ds(pl.multiple_of((p + 1) * 8, 8), 8), :]
            tile_next = cleared(ahead, p, pivot)
            pivot_next = pivot_panel(tile_next, p + 1)
        update = outer(jnp.where(lane < 8 * p, -tile, tile), pivot)
        t[...] = jnp.where(lanes // 8 == p, 0.0, t[...]) - update
        t[pl.ds(pl.multiple_of(p * 8, 8), 8), :] = pivot
        return None if last else (tile_next, pivot_next)

    first = t[0:8, :]
    held = lax.fori_loop(
        0, n - 1, lambda p, v: step(p, *v, False), (first, pivot_panel(first, 0)), unroll=15
    )
    step(n - 1, *held, True)


def between_halves(system, t, first, right, down):
    first[...] = t[...]
    right[...] = dot(t[...], system[0:128, 128:256])
    down[...] = dot(system[128:256, 0:128], t[...])
    t[...] = system[128:256, 128:256] - dot(system[128:256, 0:128], right[...])


def after_halves(t, first, right, down, inverse):
    d = t[...]
    v, vt = dot(right[...], d), dot(d, down[...])
    inverse[0:128, 0:128] = first[...] + dot(v, down[...])
    inverse[0:128, 128:256] = -v
    inverse[128:256, 0:128] = -vt
    inverse[128:256, 128:256] = d


def dot_first(left, right):
    return lax.dot_general(
        left, right, (((0,), (0,)), ((), ())), precision=highest, preferred_element_type=f32
    )


def sweep(
    nz, nc, tensor_in, factor_b_in, factor_c_in, new_a, new_b, new_c,
    tensor, factor_b, factor_c, tensor_t, gram_c, block_b, partial, landed, owned, grams,
    out_m, in_m, rows_m, rows_a, ring_m, block_m, contracted, out_b, near_b, part_b, far_b, rows_b,
    out_c, in_c, half_c, ring_c, side_c, system, half, first, right, down, inverse, scale_a, scale_b, sent, received, loaded,
):
    nq, nk = nc // 2, nz // 4
    z, c = lax.axis_index("row"), lax.axis_index("col")
    q, core = c // 2, c % 2
    class_z, place_z = z % 4, z // 4

    barrier = pltpu.get_barrier_semaphore()
    for k in sorted(range(1, nz), key=lambda k: -min(k, nz - k)):
        pl.semaphore_signal(barrier, inc=1, device_id=(lax.rem(z + k, nz), c), device_id_type=MESH)
    for k in range(1, nc):
        pl.semaphore_signal(barrier, inc=1, device_id=(z, lax.rem(c + k, nc)), device_id_type=MESH)
    loads = [
        pltpu.make_async_copy(src, dst, loaded.at[i])
        for i, (src, dst) in enumerate(((factor_b_in, factor_b), (tensor_in, tensor), (factor_c_in, factor_c)))
    ]
    for load in loads:
        load.start()
    members, wide_a, wide_b = tensor.shape
    rank = factor_b.shape[1]
    pl.semaphore_wait(barrier, nz - 1 + nc - 1)

    def copy(which, src, dst, to):
        return pltpu.make_async_remote_copy(
            src_ref=src, dst_ref=dst, send_sem=sent.at[which], recv_sem=received.at[which],
            device_id=to, device_id_type=MESH,
        )

    totals = {}

    def hops(k):
        return -(min(k % 4, 4 - k % 4) + min(k // 4, 4 - k // 4))

    def view(place):
        return place[0].at[place[1:]] if isinstance(place, tuple) else place

    def over(which, place, *blocks):
        totals[which] = lambda: view(place).at[blocks]

    def arrived(which, offset=0):
        if which in totals:
            whole = totals[which]()
            copy(which + offset, whole, whole, (z, c)).wait_recv()

    def left(which):
        whole = totals[which]()
        copy(which, whole, whole, (z, c)).wait_send()

    def send_all_z(which, src, dst):
        for k in sorted(range(1, nz), key=lambda k: -min(k, nz - k)):
            copy(which, src, dst.at[z], (lax.rem(z + k, nz), c)).start()
        over(which, dst, pl.ds(0, nz - 1))
        dst[z] = src[...]

    def send_q(which, src, place, scatter=False):
        dst = view(place)
        for k in sorted(range(1, nq), key=hops):
            other = lax.rem(q + k, nq)
            copy(which, src.at[2 * other + core] if scatter else src, dst.at[q], (z, 2 * other + core)).start()
        if nq > 1:
            over(which, place, pl.ds(0, nq - 1))
        dst[q] = src[c] if scatter else src[...]

    def send_c(which, src, place, pick=None):
        dst = view(place)
        for k in sorted(range(1, nc), key=lambda k: hops(k // 2)):
            other = lax.rem(c + k, nc)
            copy(which, src.at[pick(other)] if pick else src, dst.at[c], (z, other)).start()
        over(which, place, pl.ds(0, nc - 1))
        dst[c] = src[pick(c)] if pick else src[...]

    def sum_of(ref):
        total = ref[0]
        for k in range(1, ref.shape[0]):
            total = total + ref[k]
        return total

    far = sorted(range(1, nk), key=lambda k: -min(k, nk - k))

    def to_near(which, block):
        for k in (2, 1, nz - 1):
            copy(which, block, block, (lax.rem(z + k, nz), c)).start()

    def gather_start(which, src, place):
        dst = view(place)
        for k in far:
            copy(which + k, src, dst.at[class_z, place_z], (lax.rem(z + 4 * k, nz), c)).start()
            over(which + k, place, 0, 0)
        dst[class_z, place_z] = src[...]
        to_near(which, dst.at[class_z, place_z])
        over(which, place, pl.ds(0, 3), 0)

    def gather_on(which, place):
        dst = view(place)
        for k in reversed(far):
            arrived(which + k)
            to_near(which + nk - 1 + k, dst.at[class_z, lax.rem(place_z + nk - k, nk)])
            over(which + nk - 1 + k, place, pl.ds(0, 3), 0)

    def gather_end(which):
        arrived(which)
        for k in reversed(far):
            arrived(which + nk - 1 + k)

    def gathered(ref):
        return jnp.concatenate([ref[k % 4, k // 4] for k in range(nz)], axis=0)

    def scatter_near(which, src, dst, place):
        for slot, k in enumerate((1, nz - 1, 2)):
            other = lax.rem(z + k, nz)
            copy(which + place, src.at[lax.rem(z + k, 4), place], dst.at[slot, place], (other, c)).start()

    def scatter_far(which, src, dst, k):
        place = lax.rem(place_z + k, nk)
        copy(which, src.at[place], dst.at[k - 1], (lax.rem(z + 4 * k, nz), c)).start()

    part = rank // nc

    def gram_start(turn, block, both):
        partial[turn] = dot_first(block, block).reshape(nc, part, rank)
        if both:
            send_c(3 * turn, partial.at[turn], (landed, turn), lambda other: other)
        else:
            send_q(3 * turn, partial.at[turn], (landed, turn, pl.ds(0, nq)), True)

    def gram_middle(turn, both):
        arrived(3 * turn)
        owned[turn] = sum_of(landed.at[turn] if both else landed.at[turn, pl.ds(0, nq)])
        send_c(3 * turn + 1, owned.at[turn], (grams, turn))

    def gram_of(turn):
        arrived(3 * turn + 1)
        return grams[turn].reshape(rank, rank)

    def scales(gram, count):
        one = lax.broadcasted_iota(jnp.int32, gram.shape, 0) == lax.broadcasted_iota(jnp.int32, gram.shape, 1)
        diagonal = jnp.where(one, gram, 0.0)
        return (
            jnp.sqrt(jnp.sum(diagonal, axis=0, keepdims=True) / count + epsilon),
            jnp.sqrt(jnp.sum(diagonal, axis=1, keepdims=True) / count + epsilon),
        )

    def stage(i, carry):
        @pl.when(i == 0)
        def _():
            loads[0].wait()
            gather_start(18, factor_b, (block_b, 0))
            loads[1].wait()
            loads[2].wait()
            for m in range(members):
                tensor_t[:, m * wide_a : (m + 1) * wide_a] = jnp.transpose(tensor[m])
            by_row = factor_c[...]
            gram_c[...] = dot_first(by_row, by_row)
            gather_on(18, (block_b, 0))
            gather_end(18)
            whole_b = gathered(block_b.at[0])
            gram_start(0, whole_b, True)
            products = dot(tensor[...].reshape(members * wide_a, wide_b), whole_b).reshape(members, wide_a, rank)
            sums = products[0] * by_row[0:1]
            for m in range(1, members):
                sums = sums + products[m] * by_row[m : m + 1]
            out_m[...] = sums.reshape(nq, 8, rank)
            send_c(9, out_m, in_m, lambda other: other // 2)
            gram_middle(0, True)
            arrived(9)
            rows_m[...] = sum_of(in_m)
            send_all_z(10, rows_m, ring_m)
            send_q(11, rows_m, block_m)
            system[...] = gram_of(0) * gram_c[...]
            half[...] = system[0:128, 0:128]

        @pl.when(jnp.logical_and(i > 0, i % 2 == 0))
        def _():
            after_halves(half, first, right, down, inverse)

        @pl.when(i == 2)
        def _():
            arrived(11)
            by_row = factor_c[...]
            whole_a = dot(block_m[...].reshape(wide_a, rank), inverse[...])
            weighted = jnp.concatenate([whole_a * by_row[m : m + 1] for m in range(members)], axis=0)
            deep = wide_b // nk
            for k in far + [0]:
                place = lax.rem(place_z + k, nk)
                rows = pl.ds(pl.multiple_of(place * deep, 8), deep)
                out_b[:, place] = dot(tensor_t[rows, :], weighted).reshape(4, -1, rank)
                scatter_near(32, out_b, near_b, place)
            for k in range(nk):
                over(32 + k, near_b, pl.ds(0, 3), 0)
            arrived(10)
            gram_start(1, dot(ring_m[...].reshape(nz * 8, rank), inverse[...]), False)
            for m in range(members):
                contracted[m] = dot(tensor_t[:, m * wide_a : (m + 1) * wide_a], whole_a)
            rows_a[...] = dot(rows_m[...], inverse[...])
            for k in far + [0]:
                place = lax.rem(place_z + k, nk)
                arrived(32, place)
                part_b[place] = (out_b[class_z, place] + near_b[0, place]) + (near_b[1, place] + near_b[2, place])
                if k:
                    scatter_far(13, part_b, far_b, k)
            if nk > 1:
                over(13, far_b, pl.ds(0, nk - 1))
            gram_middle(1, False)
            arrived(13)
            total = part_b[place_z]
            for k in range(nk - 1):
                total = total + far_b[k]
            rows_b[...] = total
            gather_start(25, rows_b, (block_b, 1))
            gram = gram_of(1)
            across, along = scales(gram, wide_a * nz)
            scale_a[...] = across
            gram_a = gram / (across * along)
            system[...] = gram_a * gram_c[...]
            gram_c[...] = gram_a
            own = rows_a[...] / across
            new_a[...] = jnp.where(core == 0, own[0:4], own[4:8])
            half[...] = system[0:128, 0:128]

        @pl.when(i == 3)
        def _():
            gather_on(25, (block_b, 1))

        @pl.when(i == 4)
        def _():
            per_scale_a = 1.0 / scale_a[...]
            for m in range(members):
                contracted[m] = contracted[m] * per_scale_a
            raw_b_own = dot(rows_b[...] * per_scale_a, inverse[...])
            gather_end(25)

            raw_b = dot(gathered(block_b.at[1]) * per_scale_a, inverse[...])
            gram_start(2, raw_b, True)
            sums = jnp.concatenate(
                [jnp.sum(contracted[m] * raw_b, axis=0, keepdims=True) for m in range(members)], axis=0
            )
            out_c[0] = sums[:, 0:128]
            out_c[1] = sums[:, 128:256]
            send_c(16, out_c, in_c, lambda other: other % 2)
            gram_middle(2, True)
            arrived(16)
            half_c[...] = sum_of(in_c)
            send_all_z(17, half_c, ring_c)
            gram = gram_of(2)
            across, along = scales(gram, wide_b * nc)
            scale_b[...] = across
            system[...] = gram_c[...] * (gram / (across * along))
            new_b[...] = raw_b_own / across
            half[...] = system[0:128, 0:128]

        @pl.when(i == 5)
        def _():
            arrived(17)
            side_c[core] = sum_of(ring_c)
            copy(15, side_c.at[core], side_c.at[core], (z, c + 1 - 2 * core)).start()
            over(15, side_c, 0)

        @pl.when(i % 2 == 1)
        def _():
            between_halves(system, half, first, right, down)

        invert_half(half)
        return carry

    lax.fori_loop(0, 6, stage, 0)
    after_halves(half, first, right, down, inverse)
    arrived(15)
    new_c[...] = dot(jnp.concatenate([side_c[0], side_c[1]], axis=1) / scale_b[...], inverse[...])
    for which in totals:
        left(which)


def solution(mesh):
    nz, nc = mesh.shape["row"], mesh.shape["col"]
    nq, nk = nc // 2, nz // 4

    def on_device(tensor, factor_b, factor_c):
        members, wide_a, wide_b = tensor.shape
        deep_b, rank = factor_b.shape
        part = rank // nc
        memory = [
            tensor.shape,
            factor_b.shape,
            factor_c.shape,
            (wide_b, members * wide_a),
            (rank, rank),
            (2, 4, nk, deep_b, rank),
            (3, nc, part, rank),
            (3, nc, part, rank),
            (3, part, rank),
            (3, nc, part, rank),
            (nq, 8, rank),
            (nc, 8, rank),
            (8, rank),
            (8, rank),
            (nz, 8, rank),
            (nq, 8, rank),
            (members, wide_b, rank),
            (4, nk, deep_b, rank),
            (3, nk, deep_b, rank),
            (nk, deep_b, rank),
            (max(nk - 1, 1), deep_b, rank),
            (deep_b, rank),
            (2, members, 128),
            (nc, members, 128),
            (members, 128),
            (nz, members, 128),
            (2, members, 128),
            (rank, rank),
            (128, 128),
            (128, 128),
            (128, 128),
            (128, 128),
            (rank, rank),
            (1, rank),
            (1, rank),
        ]
        return pl.pallas_call(
            functools.partial(sweep, nz, nc),
            out_shape=(
                jax.ShapeDtypeStruct((wide_a // nc, rank), f32),
                jax.ShapeDtypeStruct((deep_b, rank), f32),
                jax.ShapeDtypeStruct((members, rank), f32),
            ),
            in_specs=[pl.BlockSpec(memory_space=pltpu.HBM)] * 3,
            out_specs=tuple([pl.BlockSpec(memory_space=pltpu.VMEM)] * 3),
            scratch_shapes=[pltpu.VMEM(shape, f32) for shape in memory]
            + [pltpu.SemaphoreType.DMA((EXCHANGES,)), pltpu.SemaphoreType.DMA((EXCHANGES,))]
            + [pltpu.SemaphoreType.DMA((3,))],
            compiler_params=pltpu.CompilerParams(
                collective_id=0, has_side_effects=True, vmem_limit_bytes=40 * 1024 * 1024
            ),
        )(tensor, factor_b, factor_c)

    return jax.shard_map(
        on_device,
        mesh=mesh,
        in_specs=(P(None, "row", "col"), P("row", "col"), P()),
        out_specs=(P(("row", "col"), None), P("row", "col"), P()),
        check_vma=False,
    )
```

time: 105 us -> 100 us (0.952)
  Pallas kernels: 99.9 us -> 94.8 us
    pallas_call x1, Pallas kernels: 99.9 us -> 94.8 us  [on_device(): pl.pallas_call(functools.partial(sweep, nz, nc), out_shape=(jax.ShapeDtyp...]
where the time goes in v4:
time: 100 us; the launch traced here: 99.9 us
  Pallas kernels  94.8 us (95%)
  local copies, waits for them, and re-layouts  4.43 us (4%)
    pallas_call x1, Pallas kernels, on_device(): pl.pallas_call(functools.partial(sweep, nz, nc), out_shape=(jax.ShapeDtyp...  94.8 us
    unnamed x9, local copies, waits for them, and re-layouts  4.43 us

profile of v4, /device:TPU:1, one launch (start us, length us, event | category | flops | bytes accessed | tf_op | source)
XLA Modules:
  0.0 99.9 jit_solution(16128715801446199475)
XLA Ops:
  0.6 0.0 copy-start
  0.6 1.2 %copy-done = f32[8,128,256]{2,1,0:T(8,128)S(1)} copy-done((f32[8,128,256]{2,1,0:T(8,128)S(1)}, f32[8,128,256]{2,1,0:T(8,128)}, u32[]{:S(2)}) %copy-start) | copy-done | bytes 1048600
  1.9 0.0 copy-start.1
  1.9 0.7 copy-done.1
  2.6 0.0 copy-start.2
  2.6 0.7 copy-done.2
  3.3 94.8 %shard_map.58 = (f32[4,256]{1,0:T(4,128)S(1)}, f32[16,256]{1,0:T(8,128)S(1)}, f32[8,256]{1,0:T(8,128)S(1)}) custom-call(f32[8,128,256]{2,1,0:T(8,128)S(1)} %copy-done, f32[16,256]{1,0:T(8,128)S(1)} %copy-done.1, f32[8,256]{1,0:T(8,128)S(1)} %copy-done.2), custom_call_target="tpu_custom_call" | custom-call | tf_op jit(solution)/shard_map/pallas_call | solution.py:437
  98.1 0.6 copy.9
  98.7 0.6 copy.10
  99.3 0.6 copy.11
Async XLA Ops:
  0.6 1.2 %copy-start = (f32[8,128,256]{2,1,0:T(8,128)S(1)}, f32[8,128,256]{2,1,0:T(8,128)}, u32[]{:S(2)}) copy-start(f32[8,128,256]{2,1,0:T(8,128)} %tensor_in.1) | copy-start | bytes 3145732
  1.9 0.7 copy-start.1
  2.6 0.7 copy-start.2

commit v5 on v4

--- a/solution.py
+++ b/solution.py
@@ -11,7 +11,7 @@
 bf16 = jnp.bfloat16
 highest = lax.Precision.HIGHEST
 epsilon = 1e-06
-EXCHANGES = 36
+EXCHANGES = 52
 MESH = pl.DeviceIdType.MESH
 
 
@@ -116,7 +116,7 @@
 def sweep(
     nz, nc, tensor_in, factor_b_in, factor_c_in, new_a, new_b, new_c,
     tensor, factor_b, factor_c, tensor_t, gram_c, block_b, partial, landed, owned, grams,
-    out_m, in_m, rows_m, rows_a, ring_m, block_m, contracted, out_b, near_b, part_b, far_b, rows_b,
+    out_m, in_m, rows_m, rows_a, ring_m, block_m, contracted, out_b, near_b, part_b, far_b, rows_b, raw_b_own,
     out_c, in_c, half_c, ring_c, side_c, system, half, first, right, down, inverse, scale_a, scale_b, sent, received, loaded,
 ):
     nq, nk = nc // 2, nz // 4
@@ -236,20 +236,27 @@
     part = rank // nc
 
     def gram_start(turn, block, both):
-        partial[turn] = dot_first(block, block).reshape(nc, part, rank)
-        if both:
-            send_c(3 * turn, partial.at[turn], (landed, turn), lambda other: other)
-        else:
-            send_q(3 * turn, partial.at[turn], (landed, turn, pl.ds(0, nq)), True)
+        whole = dot_first(block, block)
+        for side in range(2):
+            partial[turn, side] = whole[:, 128 * side : 128 * side + 128].reshape(nc, part, 128)
+            if both:
+                send_c(40 + 4 * turn + side, partial.at[turn, side], (landed, turn, side), lambda other: other)
+            else:
+                send_q(40 + 4 * turn + side, partial.at[turn, side], (landed, turn, side, pl.ds(0, nq)), True)
 
     def gram_middle(turn, both):
-        arrived(3 * turn)
-        owned[turn] = sum_of(landed.at[turn] if both else landed.at[turn, pl.ds(0, nq)])
-        send_c(3 * turn + 1, owned.at[turn], (grams, turn))
+        for side in range(2):
+            arrived(40 + 4 * turn + side)
+            owned[turn, side] = sum_of(landed.at[turn, side] if both else landed.at[turn, side, pl.ds(0, nq)])
+            send_c(42 + 4 * turn + side, owned.at[turn, side], (grams, turn, side))
+
+    def leading(turn):
+        arrived(42 + 4 * turn)
+        return grams[turn, 0, 0 : nc // 2].reshape(128, 128)
 
     def gram_of(turn):
-        arrived(3 * turn + 1)
-        return grams[turn].reshape(rank, rank)
+        arrived(43 + 4 * turn)
+        return jnp.concatenate([grams[turn, side].reshape(rank, 128) for side in range(2)], axis=1)
 
     def scales(gram, count):
         one = lax.broadcasted_iota(jnp.int32, gram.shape, 0) == lax.broadcasted_iota(jnp.int32, gram.shape, 1)
@@ -285,8 +292,11 @@
             rows_m[...] = sum_of(in_m)
             send_all_z(10, rows_m, ring_m)
             send_q(11, rows_m, block_m)
+            half[...] = leading(0) * gram_c[0:128, 0:128]
+
+        @pl.when(i == 1)
+        def _():
             system[...] = gram_of(0) * gram_c[...]
-            half[...] = system[0:128, 0:128]
 
         @pl.when(jnp.logical_and(i > 0, i % 2 == 0))
         def _():
@@ -326,6 +336,12 @@
                 total = total + far_b[k]
             rows_b[...] = total
             gather_start(25, rows_b, (block_b, 1))
+            gram = leading(1)
+            across, along = scales(gram, wide_a * nz)
+            half[...] = gram / (across * along) * gram_c[0:128, 0:128]
+
+        @pl.when(i == 3)
+        def _():
             gram = gram_of(1)
             across, along = scales(gram, wide_a * nz)
             scale_a[...] = across
@@ -334,10 +350,6 @@
             gram_c[...] = gram_a
             own = rows_a[...] / across
             new_a[...] = jnp.where(core == 0, own[0:4], own[4:8])
-            half[...] = system[0:128, 0:128]
-
-        @pl.when(i == 3)
-        def _():
             gather_on(25, (block_b, 1))
 
         @pl.when(i == 4)
@@ -345,7 +357,7 @@
             per_scale_a = 1.0 / scale_a[...]
             for m in range(members):
                 contracted[m] = contracted[m] * per_scale_a
-            raw_b_own = dot(rows_b[...] * per_scale_a, inverse[...])
+            raw_b_own[...] = dot(rows_b[...] * per_scale_a, inverse[...])
             gather_end(25)
 
             raw_b = dot(gathered(block_b.at[1]) * per_scale_a, inverse[...])
@@ -360,15 +372,17 @@
             arrived(16)
             half_c[...] = sum_of(in_c)
             send_all_z(17, half_c, ring_c)
+            gram = leading(2)
+            across, along = scales(gram, wide_b * nc)
+            half[...] = gram_c[0:128, 0:128] * (gram / (across * along))
+
+        @pl.when(i == 5)
+        def _():
             gram = gram_of(2)
             across, along = scales(gram, wide_b * nc)
             scale_b[...] = across
             system[...] = gram_c[...] * (gram / (across * along))
-            new_b[...] = raw_b_own / across
-            half[...] = system[0:128, 0:128]
-
-        @pl.when(i == 5)
-        def _():
+            new_b[...] = raw_b_own[...] / across
             arrived(17)
             side_c[core] = sum_of(ring_c)
             copy(15, side_c.at[core], side_c.at[core], (z, c + 1 - 2 * core)).start()
@@ -404,10 +418,10 @@
             (wide_b, members * wide_a),
             (rank, rank),
             (2, 4, nk, deep_b, rank),
-            (3, nc, part, rank),
-            (3, nc, part, rank),
-            (3, part, rank),
-            (3, nc, part, rank),
+            (3, 2, nc, part, 128),
+            (3, 2, nc, part, 128),
+            (3, 2, part, 128),
+            (3, 2, nc, part, 128),
             (nq, 8, rank),
             (nc, 8, rank),
             (8, rank),
@@ -419,6 +433,7 @@
             (3, nk, deep_b, rank),
             (nk, deep_b, rank),
             (max(nk - 1, 1), deep_b, rank),
+            (deep_b, rank),
             (deep_b, rank),
             (2, members, 128),
             (nc, members, 128),

time: 100 us -> 98.5 us (0.985)
  Pallas kernels: 94.8 us -> 93.2 us
    pallas_call x1, Pallas kernels: 94.8 us -> 93.2 us  [on_device(): pl.pallas_call(functools.partial(sweep, nz, nc), out_shape=(jax.ShapeDtyp...]
where the time goes in v5:
time: 98.5 us; the launch traced here: 98.3 us
  Pallas kernels  93.2 us (95%)
  local copies, waits for them, and re-layouts  4.43 us (4%)
    pallas_call x1, Pallas kernels, on_device(): pl.pallas_call(functools.partial(sweep, nz, nc), out_shape=(jax.ShapeDtyp...  93.2 us
    unnamed x9, local copies, waits for them, and re-layouts  4.43 us

profile of v5, /device:TPU:1, one launch (start us, length us, event | category | flops | bytes accessed | tf_op | source)
XLA Modules:
  0.0 98.3 jit_solution(4438933188176483475)
XLA Ops:
  0.6 0.0 copy-start
  0.6 1.2 %copy-done = f32[8,128,256]{2,1,0:T(8,128)S(1)} copy-done((f32[8,128,256]{2,1,0:T(8,128)S(1)}, f32[8,128,256]{2,1,0:T(8,128)}, u32[]{:S(2)}) %copy-start) | copy-done | bytes 1048600
  1.9 0.0 copy-start.1
  1.9 0.7 copy-done.1
  2.6 0.0 copy-start.2
  2.6 0.7 copy-done.2
  3.3 93.2 %shard_map.58 = (f32[4,256]{1,0:T(4,128)S(1)}, f32[16,256]{1,0:T(8,128)S(1)}, f32[8,256]{1,0:T(8,128)S(1)}) custom-call(f32[8,128,256]{2,1,0:T(8,128)S(1)} %copy-done, f32[16,256]{1,0:T(8,128)S(1)} %copy-done.1, f32[8,256]{1,0:T(8,128)S(1)} %copy-done.2), custom_call_target="tpu_custom_call" | custom-call | tf_op jit(solution)/shard_map/pallas_call | solution.py:452
  96.5 0.6 copy.9
  97.1 0.6 copy.10
  97.7 0.6 copy.11
Async XLA Ops:
  0.6 1.2 %copy-start = (f32[8,128,256]{2,1,0:T(8,128)S(1)}, f32[8,128,256]{2,1,0:T(8,128)}, u32[]{:S(2)}) copy-start(f32[8,128,256]{2,1,0:T(8,128)} %tensor_in.1) | copy-start | bytes 3145732
  1.9 0.7 copy-start.1
  2.6 0.7 copy-start.2

commit v6 on v5

--- a/solution.py
+++ b/solution.py
@@ -318,9 +318,6 @@
                 over(32 + k, near_b, pl.ds(0, 3), 0)
             arrived(10)
             gram_start(1, dot(ring_m[...].reshape(nz * 8, rank), inverse[...]), False)
-            for m in range(members):
-                contracted[m] = dot(tensor_t[:, m * wide_a : (m + 1) * wide_a], whole_a)
-            rows_a[...] = dot(rows_m[...], inverse[...])
             for k in far + [0]:
                 place = lax.rem(place_z + k, nk)
                 arrived(32, place)
@@ -329,6 +326,9 @@
                     scatter_far(13, part_b, far_b, k)
             if nk > 1:
                 over(13, far_b, pl.ds(0, nk - 1))
+            for m in range(members):
+                contracted[m] = dot(tensor_t[:, m * wide_a : (m + 1) * wide_a], whole_a)
+            rows_a[...] = dot(rows_m[...], inverse[...])
             gram_middle(1, False)
             arrived(13)
             total = part_b[place_z]
@@ -462,7 +462,7 @@
             + [pltpu.SemaphoreType.DMA((EXCHANGES,)), pltpu.SemaphoreType.DMA((EXCHANGES,))]
             + [pltpu.SemaphoreType.DMA((3,))],
             compiler_params=pltpu.CompilerParams(
-                collective_id=0, has_side_effects=True, vmem_limit_bytes=40 * 1024 * 1024
+                collective_id=0, has_side_effects=True, vmem_limit_bytes=64 * 1024 * 1024 - 524288
             ),
         )(tensor, factor_b, factor_c)
 

time: 98.5 us -> 97.8 us (level)
  local copies, waits for them, and re-layouts: 4.43 us -> 3.2 us
    unnamed x9 -> x7, local copies, waits for them, and re-layouts: 4.43 us -> 3.2 us
where the time goes in v6:
time: 97.8 us; the launch traced here: 97.6 us
  Pallas kernels  93.7 us (96%)
  local copies, waits for them, and re-layouts  3.2 us (3%)
    pallas_call x1, Pallas kernels, on_device(): pl.pallas_call(functools.partial(sweep, nz, nc), out_shape=(jax.ShapeDtyp...  93.7 us
    unnamed x7, local copies, waits for them, and re-layouts  3.2 us

profile of v6, /device:TPU:1, one launch (start us, length us, event | category | flops | bytes accessed | tf_op | source)
XLA Modules:
  0.0 97.6 jit_solution(9253173990454562474)
XLA Ops:
  0.6 93.7 %shard_map.58 = (f32[4,256]{1,0:T(4,128)}, f32[16,256]{1,0:T(8,128)}, f32[8,256]{1,0:T(8,128)}) custom-call(f32[8,128,256]{2,1,0:T(8,128)} %tensor_in.1, f32[16,256]{1,0:T(8,128)} %factor_b_in.1, f32[8,256]{1,0:T(8,128)} %factor_c_in.1), custom_call_target="tpu_custom_call" | custom-call | tf_op jit(solution)/shard_map/pallas_call | solution.py:452
  94.4 0.0 copy-start.1
  94.4 0.7 copy-done.1
  95.1 0.6 copy.9
  95.6 0.0 copy-start
  95.7 1.3 %copy.10 = f32[16,256]{1,0:T(8,128)} copy(f32[16,256]{1,0:T(8,128)} %get-tuple-element.7) | data formatting | bytes 32768
  97.0 0.0 copy-done
  97.0 0.6 copy.11
Async XLA Ops:
  94.4 0.7 copy-start.1
  95.6 1.3 %copy-start = (f32[8,256]{1,0:T(8,128)S(1)}, f32[8,256]{1,0:T(8,128)}, u32[]{:S(2)}) copy-start(f32[8,256]{1,0:T(8,128)} %get-tuple-element.8) | copy-start | bytes 24580
